TPU v7x, 512 devices: a whole 4x8x8 slice. The times are simulated.
512 devices in a mesh: ab: 32 (over x_lo, y, core), cd: 16 (over x_hi, z).
Axes of the slice: x: 4 (x_hi: 2, x_lo: 2; x = x_hi * 2 + x_lo), y: 8, z: 8, core: 2. Of those that a mesh axis runs over, the one named last changes fastest.
Arguments:
- integrals: bfloat16 [12800, 83200], P('ab', 'cd'), may hold values from -0.0390625 to 0.0390625
- doubles: bfloat16 [2048, 83200], P('ab', 'cd'), may hold values from -6 to 6
- singles: float32 [160, 400], replicated, may hold values from -6 to 6
Outputs:
- ladder: float32 [8, 12800, 64], P(None, ('ab', 'cd'))
All inputs are finite; a program needn't handle non-finite values.
Results may differ from a plain program's by a relative error of at most 0.0029.
Values may be sent and summed in bfloat16 or wider, within the bound.
A program may use at most 64 MiB of HBM per device.

v0:
```python
import jax
import jax.numpy as jnp
from jax import lax
from jax.sharding import PartitionSpec as P


def passed_along(array, axis, by):
    length = lax.axis_size(axis)
    return lax.ppermute(array, axis, [(i, (i + by) % length) for i in range(length)])


def contract(integrals, taken):
    return lax.dot_general(
        integrals, taken, (((1,), (1,)), ((), ())), preferred_element_type=jnp.float32
    )


def shards(integrals, doubles, singles):
    ab_count = lax.axis_size("ab")
    steps_total = ab_count // 4
    lead = steps_total // 2 - 1
    offsets = [position - lead for position in range(steps_total)]
    row_count, column_count = integrals.shape
    pair_count = doubles.shape[0]
    occupied, virtual = singles.shape
    c_local = column_count // virtual
    pair_ids = lax.axis_index("ab") * pair_count + jnp.arange(pair_count, dtype=jnp.int32)
    left_rows = jnp.take(singles, pair_ids // occupied, axis=0)
    left_cols = lax.dynamic_slice_in_dim(left_rows, lax.axis_index("cd") * c_local, c_local, 1)
    right_rows = jnp.take(singles, pair_ids % occupied, axis=0)
    amplitude = (
        doubles.reshape(pair_count, c_local, virtual).astype(jnp.float32)
        + left_cols[:, :, None] * right_rows[:, None, :]
    )
    tau_own = amplitude.reshape(pair_count, column_count).astype(jnp.bfloat16)
    held = {}
    moving = passed_along(tau_own, "ab", -lead)
    for position in range(steps_total):
        held[offsets[position]] = moving
        if position + 1 < steps_total:
            moving = passed_along(moving, "ab", 1)
    results = []
    for offset in offsets:
        results.append(
            lax.psum_scatter(
                contract(integrals, held[offset]), "cd", scatter_dimension=0, tiled=True
            )
        )
    ladder = jnp.stack(results)
    return ladder


def solution(mesh):
    in_specs = (P("ab", "cd"), P("ab", "cd"), P())
    out_specs = P(None, ("ab", "cd"), None)
    return jax.shard_map(shards, mesh=mesh, in_specs=in_specs, out_specs=out_specs, check_vma=False)
```

profile of v0, /device:TPU:6, one launch (start us, length us, event | category | flops | bytes accessed | tf_op | source)
XLA Modules:
  0.0 321.8 jit_solution(11977548558156576005)
XLA Ops:
  6.6 0.9 copy-done
  7.5 0.7 gather_fusion.1
  8.2 0.7 gather_fusion
  8.8 0.1 broadcast_select_fusion
  8.9 0.1 dynamic-slice_select_fusion
  9.0 0.2 broadcast_multiply_fusion
  9.2 2.0 mul.28
  11.2 1.6 add_convert_fusion
  12.8 6.0 %collective-permute-start = (bf16[64,5200]{1,0:T(8,128)(2,1)S(1)}, bf16[64,5200]{1,0:T(8,128)(2,1)S(1)}, u32[]{:S(2)}, u32[]{:S(2)}) collective-permute-start(bf16[64,5200]{1,0:T(8,128)(2,1)S(1)} %add_convert_fusion), channel_id=1, source_target_pairs={{0,464},{16,480},{32,496},{48,0},{64,16},{80,32},{96,48},{112,64},... | collective-permute-start | bytes 1996808 | tf_op jit(solution)/shard_map/ppermute | solution.py:9
  18.8 21.9 %collective-permute-done = bf16[64,5200]{1,0:T(8,128)(2,1)S(1)} collective-permute-done((bf16[64,5200]{1,0:T(8,128)(2,1)S(1)}, bf16[64,5200]{1,0:T(8,128)(2,1)S(1)}, u32[]{:S(2)}, u32[]{:S(2)}) %collective-permute-start) | collective-permute-done | bytes 665632 | tf_op jit(solution)/shard_map/ppermute | solution.py:9
  40.7 1.9 collective-permute-start.1
  42.6 12.3 %collective-permute-done.1 = bf16[64,5200]{1,0:T(8,128)(2,1)S(1)} collective-permute-done((bf16[64,5200]{1,0:T(8,128)(2,1)S(1)}, bf16[64,5200]{1,0:T(8,128)(2,1)S(1)}, u32[]{:S(2)}, u32[]{:S(2)}) %collective-permute-start.1) | collective-permute-done | bytes 665632 | tf_op jit(solution)/shard_map/ppermute | solution.py:9
  54.9 1.9 collective-permute-start.2
  56.8 12.3 %collective-permute-done.2 = bf16[64,5200]{1,0:T(8,128)(2,1)S(1)} collective-permute-done((bf16[64,5200]{1,0:T(8,128)(2,1)S(1)}, bf16[64,5200]{1,0:T(8,128)(2,1)S(1)}, u32[]{:S(2)}, u32[]{:S(2)}) %collective-permute-start.2) | collective-permute-done | bytes 665632 | tf_op jit(solution)/shard_map/ppermute | solution.py:9
  69.0 1.9 collective-permute-start.3
  71.0 12.3 %collective-permute-done.3 = bf16[64,5200]{1,0:T(8,128)(2,1)S(1)} collective-permute-done((bf16[64,5200]{1,0:T(8,128)(2,1)S(1)}, bf16[64,5200]{1,0:T(8,128)(2,1)S(1)}, u32[]{:S(2)}, u32[]{:S(2)}) %collective-permute-start.3) | collective-permute-done | bytes 665632 | tf_op jit(solution)/shard_map/ppermute | solution.py:9
  83.2 1.9 collective-permute-start.4
  85.1 4.2 %convolution_bitcast_fusion.7 = f32[400,64]{0,1:T(8,128)} fusion(bf16[64,5200]{1,0:T(8,128)(2,1)S(1)} %collective-permute-done, bf16[400,5200]{1,0:T(8,128)(2,1)} %param.5), kind=kOutput, calls=%fused_computation.10 | convolution fusion | flops 266240000 | bytes 4928000 | tf_op jit(solution)/shard_map/dot_general | solution.py:13
  89.3 8.1 %collective-permute-done.4 = bf16[64,5200]{1,0:T(8,128)(2,1)S(1)} collective-permute-done((bf16[64,5200]{1,0:T(8,128)(2,1)S(1)}, bf16[64,5200]{1,0:T(8,128)(2,1)S(1)}, u32[]{:S(2)}, u32[]{:S(2)}) %collective-permute-start.4) | collective-permute-done | bytes 665632 | tf_op jit(solution)/shard_map/ppermute | solution.py:9
  97.4 1.9 collective-permute-start.5
  99.3 2.0 convolution_bitcast_fusion.6
  101.3 2.0 convolution_bitcast_fusion.5
  103.3 8.2 %collective-permute-done.5 = bf16[64,5200]{1,0:T(8,128)(2,1)S(1)} collective-permute-done((bf16[64,5200]{1,0:T(8,128)(2,1)S(1)}, bf16[64,5200]{1,0:T(8,128)(2,1)S(1)}, u32[]{:S(2)}, u32[]{:S(2)}) %collective-permute-start.5) | collective-permute-done | bytes 665632 | tf_op jit(solution)/shard_map/ppermute | solution.py:9
  111.6 1.9 collective-permute-start.6
  113.5 2.0 convolution_bitcast_fusion.4
  115.5 2.0 convolution_bitcast_fusion.3
  117.5 8.2 %collective-permute-done.6 = bf16[64,5200]{1,0:T(8,128)(2,1)S(1)} collective-permute-done((bf16[64,5200]{1,0:T(8,128)(2,1)S(1)}, bf16[64,5200]{1,0:T(8,128)(2,1)S(1)}, u32[]{:S(2)}, u32[]{:S(2)}) %collective-permute-start.6) | collective-permute-done | bytes 665632 | tf_op jit(solution)/shard_map/ppermute | solution.py:9
  125.7 1.9 collective-permute-start.7
  127.7 2.0 convolution_bitcast_fusion.2
  129.7 2.0 convolution_bitcast_fusion.1
  131.7 8.2 %collective-permute-done.7 = bf16[64,5200]{1,0:T(8,128)(2,1)S(1)} collective-permute-done((bf16[64,5200]{1,0:T(8,128)(2,1)S(1)}, bf16[64,5200]{1,0:T(8,128)(2,1)S(1)}, u32[]{:S(2)}, u32[]{:S(2)}) %collective-permute-start.7) | collective-permute-done | bytes 665632 | tf_op jit(solution)/shard_map/ppermute | solution.py:9
  139.9 2.0 convolution_bitcast_fusion
  142.0 1.3 dynamic-slice
  143.9 162.3 %all-reduce.11.cloned.1.call-done = (f32[400,64]{0,1:T(8,128)}, f32[400,64]{0,1:T(8,128)}, f32[400,64]{0,1:T(8,128)}, f32[400,64]{0,1:T(8,128)}, f32[400,64]{0,1...) async-done(((f32[400,64]{0,1:T(8,128)}, f32[400,64]{0,1:T(8,128)}, f32[400,64]{0,1:T(8,128)}, f32[400,64]{0,1:T(8,128)}, f32[400,64]{0,1:T(8,128)}, ...) | async-done | bytes 819216
  306.2 0.9 dynamic-slice_bitcast_fusion.7
  307.1 0.1 copy.6
  307.2 0.9 dynamic-slice_bitcast_fusion.6
  308.1 0.1 copy.7
  308.2 0.9 dynamic-slice_bitcast_fusion.5
  309.1 0.1 copy.8
  309.2 0.9 dynamic-slice_bitcast_fusion.4
  310.1 0.1 copy.9
  310.2 0.9 dynamic-slice_bitcast_fusion.3
  311.1 0.1 copy.10
  311.2 0.9 dynamic-slice_bitcast_fusion.2
  312.2 0.9 dynamic-slice_bitcast_fusion.1
  313.2 0.9 dynamic-slice_bitcast_fusion
  314.2 0.8 stack.35
  (17 shorter events, 0.3 us)
Async XLA Ops:
  6.5 1.0 copy-start
  6.5 299.6 %all-reduce.11.cloned.1.call-start = ((), (), s32[]{:S(2)}) async-start(), calls=%async_computation | async-start | bytes 2097152
  7.5 3.7 %copy-start.1 = (bf16[64,5200]{1,0:T(8,128)(2,1)S(1)}, bf16[64,5200]{1,0:T(8,128)(2,1)}, u32[]{:S(2)}) copy-start(bf16[64,5200]{1,0:T(8,128)(2,1)} %param.6) | copy-start | bytes 1996804
  9.2 90.1 %slice-start = ((s8[4198400]{0:T(1024)(128)(4,1)}), s8[4096]{0:T(1024)(128)(4,1)S(1)}, s32[]{:S(2)}) async-start(s8[4198400]{0:T(1024)(128)(4,1)} %bitcast.65), calls=%async_computation.1 | async-start | bytes 8192
  11.2 88.1 %slice-start.1 = ((s8[4198400]{0:T(1024)(128)(4,1)}), s8[4194304]{0:T(1024)(128)(4,1)S(1)}, s32[]{:S(2)}) async-start(s8[4198400]{0:T(1024)(128)(4,1)} %bitcast.65), calls=%async_computation.2 | async-start | bytes 8388608
  12.8 27.9 %collective-permute-start = (bf16[64,5200]{1,0:T(8,128)(2,1)S(1)}, bf16[64,5200]{1,0:T(8,128)(2,1)S(1)}, u32[]{:S(2)}, u32[]{:S(2)}) collective-permute-start(bf16[64,5200]{1,0:T(8,128)(2,1)S(1)} %add_convert_fusion), channel_id=1, source_target_pairs={{0,464},{16,480},{32,496},{48,0},{64,16},{80,32},{96,48},{112,64},... | collective-permute-start | bytes 1996808 | tf_op jit(solution)/shard_map/ppermute | solution.py:9
  40.7 14.2 %collective-permute-start.1 = (bf16[64,5200]{1,0:T(8,128)(2,1)S(1)}, bf16[64,5200]{1,0:T(8,128)(2,1)S(1)}, u32[]{:S(2)}, u32[]{:S(2)}) collective-permute-start(bf16[64,5200]{1,0:T(8,128)(2,1)S(1)} %collective-permute-done), channel_id=1, source_target_pairs={{0,16},{16,32},{32,48},{48,64},{64,80},{80,96},{96,112},{112,128},... | collective-permute-start | bytes 1996808 | tf_op jit(solution)/shard_map/ppermute | solution.py:9
  54.9 14.2 %collective-permute-start.2 = (bf16[64,5200]{1,0:T(8,128)(2,1)S(1)}, bf16[64,5200]{1,0:T(8,128)(2,1)S(1)}, u32[]{:S(2)}, u32[]{:S(2)}) collective-permute-start(bf16[64,5200]{1,0:T(8,128)(2,1)S(1)} %collective-permute-done.1), channel_id=1, source_target_pairs={{0,16},{16,32},{32,48},{48,64},{64,80},{80,96},{96,112},{112,128},... | collective-permute-start | bytes 1996808 | tf_op jit(solution)/shard_map/ppermute | solution.py:9
  69.0 14.2 %collective-permute-start.3 = (bf16[64,5200]{1,0:T(8,128)(2,1)S(1)}, bf16[64,5200]{1,0:T(8,128)(2,1)S(1)}, u32[]{:S(2)}, u32[]{:S(2)}) collective-permute-start(bf16[64,5200]{1,0:T(8,128)(2,1)S(1)} %collective-permute-done.2), channel_id=1, source_target_pairs={{0,16},{16,32},{32,48},{48,64},{64,80},{80,96},{96,112},{112,128},... | collective-permute-start | bytes 1996808 | tf_op jit(solution)/shard_map/ppermute | solution.py:9
  83.2 14.2 %collective-permute-start.4 = (bf16[64,5200]{1,0:T(8,128)(2,1)S(1)}, bf16[64,5200]{1,0:T(8,128)(2,1)S(1)}, u32[]{:S(2)}, u32[]{:S(2)}) collective-permute-start(bf16[64,5200]{1,0:T(8,128)(2,1)S(1)} %collective-permute-done.3), channel_id=1, source_target_pairs={{0,16},{16,32},{32,48},{48,64},{64,80},{80,96},{96,112},{112,128},... | collective-permute-start | bytes 1996808 | tf_op jit(solution)/shard_map/ppermute | solution.py:9
  97.4 14.2 %collective-permute-start.5 = (bf16[64,5200]{1,0:T(8,128)(2,1)S(1)}, bf16[64,5200]{1,0:T(8,128)(2,1)S(1)}, u32[]{:S(2)}, u32[]{:S(2)}) collective-permute-start(bf16[64,5200]{1,0:T(8,128)(2,1)S(1)} %collective-permute-done.4), channel_id=1, source_target_pairs={{0,16},{16,32},{32,48},{48,64},{64,80},{80,96},{96,112},{112,128},... | collective-permute-start | bytes 1996808 | tf_op jit(solution)/shard_map/ppermute | solution.py:9
  111.6 14.2 %collective-permute-start.6 = (bf16[64,5200]{1,0:T(8,128)(2,1)S(1)}, bf16[64,5200]{1,0:T(8,128)(2,1)S(1)}, u32[]{:S(2)}, u32[]{:S(2)}) collective-permute-start(bf16[64,5200]{1,0:T(8,128)(2,1)S(1)} %collective-permute-done.5), channel_id=1, source_target_pairs={{0,16},{16,32},{32,48},{48,64},{64,80},{80,96},{96,112},{112,128},... | collective-permute-start | bytes 1996808 | tf_op jit(solution)/shard_map/ppermute | solution.py:9
  125.7 14.2 %collective-permute-start.7 = (bf16[64,5200]{1,0:T(8,128)(2,1)S(1)}, bf16[64,5200]{1,0:T(8,128)(2,1)S(1)}, u32[]{:S(2)}, u32[]{:S(2)}) collective-permute-start(bf16[64,5200]{1,0:T(8,128)(2,1)S(1)} %collective-permute-done.6), channel_id=1, source_target_pairs={{0,16},{16,32},{32,48},{48,64},{64,80},{80,96},{96,112},{112,128},... | collective-permute-start | bytes 1996808 | tf_op jit(solution)/shard_map/ppermute | solution.py:9
Sparse Core Ops, SparseCore 0:
  142.1 164.0 all-reduce.10
where the time goes:
time: 324 us; the launch traced here: 322 us
  waiting for transfers between devices  254 us (78%)
  starting transfers between devices  19.4 us (6%)
  matrix products  18.2 us (6%)
  local copies, waits for them, and re-layouts  14.3 us (4%)
  between operations  14.2 us (4%)
    unnamed x2, waiting for transfers between devices  162 us
    ppermute x8, waiting for transfers between devices, passed_along(): lax.ppermute(array, axis, [(i, (i + by) % length) for i in range(length)])  91.4 us
    ppermute x8, starting transfers between devices, passed_along(): lax.ppermute(array, axis, [(i, (i + by) % length) for i in range(length)])  19.4 us
    dot_general x8, matrix products, contract(): lax.dot_general(integrals, taken, (((1,), (1,)), ((), ())), preferred_ele...  18.2 us
    another operation x17, local copies, waits for them, and re-layouts, shards(): ladder = jnp.stack(results)  8.83 us
  transfers between devices with their start and end apart: 9, of which 9 were waited for; matrix products, arithmetic and copies ran while one was open for 5% of the time, Pallas kernels for 0%

commit v1 on v0

v1 whole, which is shorter than its diff:
```python
import functools

import jax
import jax.numpy as jnp
from jax import lax
from jax.experimental import pallas as pl
from jax.experimental.pallas import tpu as pltpu
from jax.sharding import PartitionSpec as P

MESH = pl.DeviceIdType.MESH
F32 = jnp.float32
BF16 = jnp.bfloat16
N_Z = 8
KC = 1024


def kernel(
    a_hbm, d_hbm, s_hbm, o_ref,
    a_v, s_v, slots, rtab, ltab, acc, acc_h,
    sbuf, rbuf, xsend, xrecv, tot, hsend, hrecv,
    loc_sem, up_s, up_r, dn_s, dn_r, fu_s, fu_r, fd_s, fd_r, sib_s, sib_r,
    z_s, z_r, x_s, x_r, h_s, h_r,
):
    pairs, cols = d_hbm.shape
    rows = a_hbm.shape[0]
    occ, virt = s_hbm.shape
    c_local = cols // virt
    n_ab = lax.axis_size("ab")
    n_cd = lax.axis_size("cd")
    n_x = n_cd // N_Z
    take = rows // n_cd
    half = pairs // 2

    ab = lax.axis_index("ab")
    cd = lax.axis_index("cd")
    core = lax.rem(ab, 2)
    chip2 = ab - core
    x_hi = cd // N_Z
    z = lax.rem(cd, N_Z)

    nxt = {"ab": lax.rem(ab + 2, n_ab)}
    prv = {"ab": lax.rem(ab + n_ab - 2, n_ab)}
    sib = {"ab": ab + 1 - 2 * core}
    low = {"ab": lax.rem(ab + n_ab - 1, n_ab)}
    high = {"ab": lax.rem(ab + 1, n_ab)}

    def member(k):
        return {"cd": lax.rem(cd + k, n_cd)}

    bar = pltpu.get_barrier_semaphore()
    for peer in (nxt, prv, low, high):
        pl.semaphore_signal(bar, inc=1, device_id=peer, device_id_type=MESH)

    def greet(k, carry):
        pl.semaphore_signal(bar, inc=1, device_id=member(k), device_id_type=MESH)
        return carry

    lax.fori_loop(1, n_cd, greet, 0)

    load_s = pltpu.make_async_copy(s_hbm, s_v, loc_sem.at[0])
    load_d = pltpu.make_async_copy(d_hbm, slots.at[0, core], loc_sem.at[1])
    load_a = pltpu.make_async_copy(a_hbm, a_v, loc_sem.at[2])
    load_s.start()
    load_d.start()
    load_a.start()

    pl.semaphore_wait(bar, n_cd + 3)

    def remote(src, dst, ss, rs, dev):
        return pltpu.make_async_remote_copy(
            src_ref=src, dst_ref=dst, send_sem=ss, recv_sem=rs, device_id=dev, device_id_type=MESH
        )

    part = [pl.ds(i * half, half) for i in range(2)]
    up = [remote(d_hbm.at[q], slots.at[1, core, q], up_s.at[i], up_r.at[i], nxt) for i, q in enumerate(part)]
    dn = [remote(d_hbm.at[q], slots.at[2, core, q], dn_s.at[i], dn_r.at[i], prv) for i, q in enumerate(part)]
    fu = [remote(slots.at[1, core, q], slots.at[3, core, q], fu_s.at[i], fu_r.at[i], nxt) for i, q in enumerate(part)]
    fd = [remote(slots.at[2, core, q], slots.at[3, core, q], fd_s.at[i], fd_r.at[i], low) for i, q in enumerate(part)]
    own = remote(d_hbm, slots.at[0, core], sib_s.at[6], sib_r.at[6], sib)
    sh_up = [remote(slots.at[1, core, q], slots.at[1, core, q], sib_s.at[i], sib_r.at[i], sib) for i, q in enumerate(part)]
    sh_dn = [remote(slots.at[2, core, q], slots.at[2, core, q], sib_s.at[2 + i], sib_r.at[2 + i], sib) for i, q in enumerate(part)]
    sh_fu = [remote(slots.at[3, 1, q], slots.at[3, 1, q], sib_s.at[4 + i], sib_r.at[4 + i], sib) for i, q in enumerate(part)]

    for i in range(2):
        up[i].start()
        dn[i].start()
    own.start()

    load_s.wait()

    def spread(t, carry):
        rows_t = s_v[pl.ds(pl.multiple_of(lax.rem(32 * t, occ), 32), 32), :]
        at = pl.ds(pl.multiple_of(32 * t, 32), 32)
        for c in range(c_local):
            rtab[at, c * virt : (c + 1) * virt] = rows_t
        return carry

    lax.fori_loop(0, rtab.shape[0] // 32, spread, 0)
    few = s_v[0 : ltab.shape[0], :]
    lane = lax.broadcasted_iota(jnp.int32, few.shape, 1)
    for c in range(c_local):
        value = jnp.sum(jnp.where(lane == cd * c_local + c, few, 0.0), axis=1, keepdims=True)
        for i in range(few.shape[0]):
            ltab[i, :, c * virt : (c + 1) * virt] = jnp.broadcast_to(value[i : i + 1, :], (8, virt))

    def block(offset):
        g = lax.rem(chip2 + offset + n_ab, n_ab)
        first = g * pairs
        i0 = first // occ
        return i0, occ * (i0 + 1) - first, pl.multiple_of(lax.rem(first, occ), 32)

    def tau(slot, h, who, r0, count, ks, width):
        i0, turn, j0 = who
        raw = slots[slot, h, pl.ds(r0, count), ks].astype(F32)
        right = rtab[pl.ds(pl.multiple_of(j0 + r0, 32), count), ks]
        pair = lax.broadcasted_iota(jnp.int32, (count, width), 0) + r0
        before, after = (jnp.concatenate([ltab[i, :, ks]] * (count // 8), axis=0) for i in (i0, i0 + 1))
        left = jnp.where(pair < turn, before, after)
        return (raw + left * right).astype(BF16)

    def product(slot, whos, r0, count, out):
        def piece(ks, width):
            both = jnp.concatenate([tau(slot, h, whos[h], r0, count, ks, width) for h in range(2)], axis=0)
            return lax.dot_general(a_v[:, ks], both, (((1,), (1,)), ((), ())), preferred_element_type=F32)

        whole = cols // KC
        out[0:rows, :] = piece(pl.ds(whole * KC, cols - whole * KC), cols - whole * KC)

        def step(t, carry):
            out[0:rows, :] += piece(pl.ds(pl.multiple_of(t * KC, KC), KC), KC)
            return carry

        lax.fori_loop(0, whole, step, 0)

    def z_copy(s, k):
        to = lax.rem(z + k, N_Z)
        return remote(
            sbuf.at[s, to], rbuf.at[s, k - 1], z_s.at[s, k - 1], z_r.at[s, k - 1], {"cd": x_hi * N_Z + to}
        )

    def scatter(s):
        for j in range(n_cd):
            sbuf[s, j % N_Z, j // N_Z, :, :] = acc[j * take : j * take + 32, :].astype(sbuf.dtype)

        def send(k, carry):
            z_copy(s, k).start()
            return carry

        lax.fori_loop(1, N_Z, send, 0)

    def x_copy(s):
        return remote(xsend.at[s], xrecv.at[s], x_s.at[s], x_r.at[s], {"cd": (1 - x_hi) * N_Z + z})

    def gather(s):
        def arrive(k, carry):
            z_copy(s, k).wait_recv()
            return carry

        lax.fori_loop(1, N_Z, arrive, 0)
        for dst, xo in ((xsend, 1 - x_hi), (tot, x_hi)):
            total = sbuf[s, z, xo].astype(F32)
            for k in range(N_Z - 1):
                total = total + rbuf[s, k, xo].astype(F32)
            dst[s] = total
        x_copy(s).start()

    first_k = [3 + core, 2 + core, 5 + core, 4 + core, 1 + core, core, 7 - 7 * core, 6 + core]

    def finish(s):
        x_copy(s).wait_recv()
        value = tot[s] + xrecv[s]
        for h in range(2):
            o_ref[first_k[2 * s + h], :, :] = value[0:take, h * pairs : (h + 1) * pairs]

    top = (take + 1) // 2

    def h_copy(i, k):
        to = lax.rem(cd + k, n_cd)
        return remote(hsend.at[i, to], hrecv.at[i, k - 1], h_s.at[i, k - 1], h_r.at[i, k - 1], {"cd": to})

    def scatter_half(i):
        for j in range(n_cd):
            a = acc_h[j * take : j * take + 16, :]
            b = acc_h[j * take + top : j * take + top + 16, :]
            hsend[i, j, :, :] = jnp.concatenate([a, b], axis=1).astype(hsend.dtype)

        def send(k, carry):
            h_copy(i, k).start()
            return carry

        lax.fori_loop(1, n_cd, send, 0)

    def finish_half(i):
        def arrive(k, carry):
            h_copy(i, k).wait_recv()
            return carry

        lax.fori_loop(1, n_cd, arrive, 0)
        value = hsend[i, cd].astype(F32)
        for k in range(n_cd - 1):
            value = value + hrecv[i, k].astype(F32)
        for h in range(2):
            k = first_k[6 + h]
            o_ref[k, 0:top, i * half : (i + 1) * half] = value[0:top, h * half : (h + 1) * half]
            o_ref[k, top:take, i * half : (i + 1) * half] = value[
                0 : take - top, pairs + h * half : pairs + (h + 1) * half
            ]

    acc[rows:, :] = jnp.zeros((acc.shape[0] - rows, acc.shape[1]), F32)
    acc_h[rows:, :] = jnp.zeros((acc_h.shape[0] - rows, acc_h.shape[1]), F32)

    load_d.wait()
    load_a.wait()
    own.wait_recv()
    product(0, (block(0), block(1)), 0, pairs, acc)
    scatter(0)

    for i in range(2):
        up[i].wait_recv()
        fu[i].start()
        sh_up[i].start()
        dn[i].wait_recv()

        @pl.when(core == 0)
        def _():
            fd[i].start()

        sh_dn[i].start()
        if i == 0:
            gather(0)
    for i in range(2):
        sh_up[i].wait_recv()
    product(1, (block(-2), block(-1)), 0, pairs, acc)
    scatter(1)
    for i in range(2):
        sh_dn[i].wait_recv()
    product(2, (block(2), block(3)), 0, pairs, acc)
    scatter(2)
    finish(0)

    last = (block(jnp.where(core == 0, -4, 4)), block(-3))
    for i in range(2):
        fu[i].wait_recv()

        @pl.when(core == 1)
        def _():
            sh_fu[i].start()
            fd[i].wait_recv()

        if i == 0:
            gather(1)
            gather(2)

        @pl.when(core == 0)
        def _():
            sh_fu[i].wait_recv()

        product(3, last, i * half, half, acc_h)
        scatter_half(i)
        if i == 0:
            finish(1)
            finish(2)
    finish_half(0)
    finish_half(1)

    for i in range(2):
        up[i].wait_send()
        dn[i].wait_send()
        fu[i].wait_send()
        sh_up[i].wait_send()
        sh_dn[i].wait_send()

        @pl.when(core == 0)
        def _():
            fd[i].wait_send()

        @pl.when(core == 1)
        def _():
            sh_fu[i].wait_send()

    own.wait_send()
    for s in range(3):
        x_copy(s).wait_send()

        def sent(k, carry, s=s):
            z_copy(s, k).wait_send()
            return carry

        lax.fori_loop(1, N_Z, sent, 0)
    for i in range(2):

        def sent_half(k, carry, i=i):
            h_copy(i, k).wait_send()
            return carry

        lax.fori_loop(1, n_cd, sent_half, 0)


def shards(integrals, doubles, singles):
    rows, cols = integrals.shape
    pairs = doubles.shape[0]
    occ, virt = singles.shape
    n_ab, n_cd = lax.axis_size("ab"), lax.axis_size("cd")
    steps = n_ab // 4
    take = rows // n_cd
    dma = pltpu.SemaphoreType.DMA
    return pl.pallas_call(
        kernel,
        out_shape=jax.ShapeDtypeStruct((steps, take, pairs), F32),
        in_specs=[pl.BlockSpec(memory_space=pl.ANY)] * 3,
        out_specs=pl.BlockSpec(memory_space=pltpu.VMEM),
        scratch_shapes=[
            pltpu.VMEM((rows, cols), BF16),
            pltpu.VMEM((occ, virt), F32),
            pltpu.VMEM((4, 2, pairs, cols), BF16),
            pltpu.VMEM((occ + 32, cols), F32),
            pltpu.VMEM((16, 8, cols), F32),
            pltpu.VMEM((rows + 8, 2 * pairs), F32),
            pltpu.VMEM((rows + 8, pairs), F32),
            pltpu.VMEM((3, N_Z, n_cd // N_Z, 32, 2 * pairs), F32),
            pltpu.VMEM((3, N_Z - 1, n_cd // N_Z, 32, 2 * pairs), F32),
            pltpu.VMEM((3, 32, 2 * pairs), F32),
            pltpu.VMEM((3, 32, 2 * pairs), F32),
            pltpu.VMEM((3, 32, 2 * pairs), F32),
            pltpu.VMEM((2, n_cd, 16, 2 * pairs), BF16),
            pltpu.VMEM((2, n_cd - 1, 16, 2 * pairs), BF16),
            dma((3,)),
            dma((2,)), dma((2,)), dma((2,)), dma((2,)),
            dma((2,)), dma((2,)), dma((2,)), dma((2,)),
            dma((7,)), dma((7,)),
            dma((3, N_Z - 1)), dma((3, N_Z - 1)),
            dma((3,)), dma((3,)),
            dma((2, n_cd - 1)), dma((2, n_cd - 1)),
        ],
        compiler_params=pltpu.CompilerParams(
            collective_id=0, has_side_effects=True, vmem_limit_bytes=48 * 2**20
        ),
        cost_estimate=pl.CostEstimate(
            flops=2 * rows * cols * steps * pairs, bytes_accessed=2 * (rows + pairs) * cols, transcendentals=0
        ),
    )(integrals, doubles, singles)


def solution(mesh):
    in_specs = (P("ab", "cd"), P("ab", "cd"), P())
    out_specs = P(None, ("ab", "cd"), None)
    return jax.shard_map(shards, mesh=mesh, in_specs=in_specs, out_specs=out_specs, check_vma=False)
```

time: 324 us -> 68.7 us (0.21)
  waiting for transfers between devices: 254 us -> 0 us
  Pallas kernels: 0 us -> 62.9 us
  starting transfers between devices: 19.4 us -> 0 us
  matrix products: 18.2 us -> 0 us
  between operations: 14.2 us -> 0.01 us
  local copies, waits for them, and re-layouts: 14.3 us -> 4.96 us
    unnamed x2 -> x0, waiting for transfers between devices: 162 us -> none
    ppermute x8 -> x0, waiting for transfers between devices: 91.4 us -> none  [passed_along(): lax.ppermute(array, axis, [(i, (i + by) % length) for i in range(length)])]
    pallas_call x0 -> x1, Pallas kernels: none -> 62.9 us  [shards(): pl.pallas_call(kernel, out_shape=jax.ShapeDtypeStruct((steps, take, pairs...]
    ppermute x8 -> x0, starting transfers between devices: 19.4 us -> none  [passed_along(): lax.ppermute(array, axis, [(i, (i + by) % length) for i in range(length)])]
    dot_general x8 -> x0, matrix products: 18.2 us -> none  [contract(): lax.dot_general(integrals, taken, (((1,), (1,)), ((), ())), preferred_ele...]
    another operation x17 -> x0, local copies, waits for them, and re-layouts: 8.83 us -> none  [shards(): ladder = jnp.stack(results)]
  transfers between devices with their start and end apart: 9 -> 0, of which waited for: 9 -> 0; matrix products, arithmetic and copies ran while one was open for 5% -> 0% of each run, Pallas kernels for 0% -> 0%
where the time goes in v1:
time: 68.7 us; the launch traced here: 67.8 us
  Pallas kernels  62.9 us (92%)
  local copies, waits for them, and re-layouts  4.96 us (7%)
    pallas_call x1, Pallas kernels, shards(): pl.pallas_call(kernel, out_shape=jax.ShapeDtypeStruct((steps, take, pairs...  62.9 us
    unnamed x6, local copies, waits for them, and re-layouts  4.25 us

profile of v1, /device:TPU:6, one launch (start us, length us, event | category | flops | bytes accessed | tf_op | source)
XLA Modules:
  0.0 67.8 jit_solution(6327125492079664199)
XLA Ops:
  0.0 0.0 copy-start
  0.0 2.2 %copy-done = bf16[400,5200]{1,0:T(8,128)(2,1)S(1)} copy-done((bf16[400,5200]{1,0:T(8,128)(2,1)S(1)}, bf16[400,5200]{1,0:T(8,128)(2,1)}, u32[]{:S(2)}) %copy-start) | copy-done | bytes 4160024
  2.2 0.0 copy-start.1
  2.2 1.1 %copy-done.1 = bf16[64,5200]{1,0:T(8,128)(2,1)S(1)} copy-done((bf16[64,5200]{1,0:T(8,128)(2,1)S(1)}, bf16[64,5200]{1,0:T(8,128)(2,1)}, u32[]{:S(2)}) %copy-start.1) | copy-done | bytes 665624
  3.3 0.0 copy-start.2
  3.3 1.0 %copy-done.2 = f32[160,400]{1,0:T(8,128)S(1)} copy-done((f32[160,400]{1,0:T(8,128)S(1)}, f32[160,400]{1,0:T(8,128)}, u32[]{:S(2)}) %copy-start.2) | copy-done | bytes 256024
  4.3 62.9 %shard_map.37 = f32[8,25,64]{2,1,0:T(8,128)S(1)} custom-call(bf16[400,5200]{1,0:T(8,128)(2,1)S(1)} %copy-done, bf16[64,5200]{1,0:T(8,128)(2,1)S(1)} %copy-done.1, f32[160,400]{1,0:T(8,128)S(1)} %copy-done.2), custom_call_target="tpu_custom_call" | custom-call | flops 2129920000 | bytes 4825600 | tf_op jit(solution)/shard_map/pallas_call | solution.py:307
  67.1 0.7 %copy.4 = f32[8,25,64]{2,0,1:T(8,128)} copy(f32[8,25,64]{2,1,0:T(8,128)S(1)} %shard_map.37) | data formatting | bytes 102400 | tf_op jit(solution)/shard_map/pallas_call | solution.py:307
Async XLA Ops:
  0.0 2.2 %copy-start = (bf16[400,5200]{1,0:T(8,128)(2,1)S(1)}, bf16[400,5200]{1,0:T(8,128)(2,1)}, u32[]{:S(2)}) copy-start(bf16[400,5200]{1,0:T(8,128)(2,1)} %a_hbm.1) | copy-start | bytes 12480004
  2.2 1.1 %copy-start.1 = (bf16[64,5200]{1,0:T(8,128)(2,1)S(1)}, bf16[64,5200]{1,0:T(8,128)(2,1)}, u32[]{:S(2)}) copy-start(bf16[64,5200]{1,0:T(8,128)(2,1)} %d_hbm.1) | copy-start | bytes 1996804
  3.3 1.0 %copy-start.2 = (f32[160,400]{1,0:T(8,128)S(1)}, f32[160,400]{1,0:T(8,128)}, u32[]{:S(2)}) copy-start(f32[160,400]{1,0:T(8,128)} %s_hbm.1) | copy-start | bytes 768004

commit v2 on v1

v2 whole, which is shorter than its diff:
```python
import functools

import jax
import jax.numpy as jnp
from jax import lax
from jax.experimental import pallas as pl
from jax.experimental.pallas import tpu as pltpu
from jax.sharding import PartitionSpec as P

MESH = pl.DeviceIdType.MESH
F32 = jnp.float32
BF16 = jnp.bfloat16
N_Z = 8
KC = 1024


def kernel(
    a_hbm, d_hbm, s_hbm, o_ref,
    a_v, s_v, slots, rtab, ltab, acc, acc_l,
    sbuf, rbuf, xsend, xrecv, tot, hsend, hrecv, lsend, lrecv,
    loc_sem, up_s, up_r, dn_s, dn_r, fd_s, fd_r, f1_s, f1_r, f0_s, f0_r, sib_s, sib_r,
    z_s, z_r, x_s, x_r, h_s, h_r, l_s, l_r,
):
    pairs, cols = d_hbm.shape
    rows = a_hbm.shape[0]
    occ, virt = s_hbm.shape
    c_local = cols // virt
    n_ab = lax.axis_size("ab")
    n_cd = lax.axis_size("cd")
    n_x = n_cd // N_Z
    take = rows // n_cd
    half = pairs // 2

    ab = lax.axis_index("ab")
    cd = lax.axis_index("cd")
    core = lax.rem(ab, 2)
    chip2 = ab - core
    x_hi = cd // N_Z
    z = lax.rem(cd, N_Z)

    nxt = {"ab": lax.rem(ab + 2, n_ab)}
    prv = {"ab": lax.rem(ab + n_ab - 2, n_ab)}
    sib = {"ab": ab + 1 - 2 * core}
    low = {"ab": lax.rem(ab + n_ab - 1, n_ab)}
    high = {"ab": lax.rem(ab + 1, n_ab)}
    nxt0 = {"ab": lax.rem(chip2 + 2, n_ab)}

    bar = pltpu.get_barrier_semaphore()
    for peer in (nxt, prv, low, high):
        pl.semaphore_signal(bar, inc=1, device_id=peer, device_id_type=MESH)

    def greet(k, carry):
        pl.semaphore_signal(bar, inc=1, device_id={"cd": lax.rem(cd + k, n_cd)}, device_id_type=MESH)
        return carry

    lax.fori_loop(1, n_cd, greet, 0)

    load_s = pltpu.make_async_copy(s_hbm, s_v, loc_sem.at[0])
    load_d = pltpu.make_async_copy(d_hbm, slots.at[0, core], loc_sem.at[1])
    load_a = pltpu.make_async_copy(a_hbm, a_v, loc_sem.at[2])
    load_s.start()
    load_d.start()
    load_a.start()

    pl.semaphore_wait(bar, n_cd + 3)

    def remote(src, dst, ss, rs, dev):
        return pltpu.make_async_remote_copy(
            src_ref=src, dst_ref=dst, send_sem=ss, recv_sem=rs, device_id=dev, device_id_type=MESH
        )

    part = [pl.ds(pl.multiple_of(half * r, 32), half) for r in (core, 1 - core)]
    other = [pl.ds(pl.multiple_of(half * r, 32), half) for r in (1 - core, core)]
    up = [remote(d_hbm.at[q], slots.at[1, core, q], up_s.at[i], up_r.at[i], nxt) for i, q in enumerate(part)]
    dn = [remote(d_hbm.at[q], slots.at[2, core, q], dn_s.at[i], dn_r.at[i], prv) for i, q in enumerate(part)]
    own = remote(d_hbm, slots.at[0, core], sib_s.at[5], sib_r.at[5], sib)
    sh_up = [remote(slots.at[1, core, q], slots.at[1, core, q], sib_s.at[i], sib_r.at[i], sib) for i, q in enumerate(part)]
    sh_dn = [remote(slots.at[2, core, q], slots.at[2, core, q], sib_s.at[2 + i], sib_r.at[2 + i], sib) for i, q in enumerate(part)]
    f1 = remote(slots.at[1, 1, part[1]], slots.at[3, 1, part[1]], f1_s, f1_r, nxt)
    sh_f1 = remote(slots.at[3, 1, part[1]], slots.at[3, 1, part[1]], sib_s.at[4], sib_r.at[4], sib)
    f0 = remote(slots.at[1, 0, part[0]], slots.at[3, 0, part[0]], f0_s, f0_r.at[core], nxt0)
    f0_in = [
        remote(slots.at[1, 0, pl.ds(i * half, half)], slots.at[3, 0, pl.ds(i * half, half)], f0_s, f0_r.at[i], nxt0)
        for i in range(2)
    ]
    fd = [remote(slots.at[2, core, q], slots.at[3, core, q], fd_s.at[i], fd_r.at[i], low) for i, q in enumerate(part)]
    fd_in = [remote(slots.at[2, 0, q], slots.at[3, 0, q], fd_s.at[i], fd_r.at[i], low) for i, q in enumerate(other)]

    for i in range(2):
        up[i].start()
        dn[i].start()
        if i == 0:
            own.start()

    load_s.wait()

    def spread(t, carry):
        rows_t = s_v[pl.ds(pl.multiple_of(lax.rem(32 * t, occ), 32), 32), :]
        at = pl.ds(pl.multiple_of(32 * t, 32), 32)
        for c in range(c_local):
            rtab[at, c * virt : (c + 1) * virt] = rows_t
        return carry

    lax.fori_loop(0, rtab.shape[0] // 32, spread, 0)
    few = s_v[0 : ltab.shape[0], :]
    lane = lax.broadcasted_iota(jnp.int32, few.shape, 1)
    for c in range(c_local):
        value = jnp.sum(jnp.where(lane == cd * c_local + c, few, 0.0), axis=1, keepdims=True)
        for i in range(few.shape[0]):
            ltab[i, :, c * virt : (c + 1) * virt] = jnp.broadcast_to(value[i : i + 1, :], (8, virt))

    far = jnp.where(core == 0, -4, 4)
    place = {(0, 0): 0, (0, 1): 1, (1, 0): -2, (1, 1): -1, (2, 0): 2, (2, 1): 3, (3, 0): far, (3, 1): -3}
    first_k = {
        (0, 0): 3 + core, (0, 1): 2 + core, (1, 0): 5 + core, (1, 1): 4 + core,
        (2, 0): 1 + core, (2, 1): core, (3, 0): 7 - 7 * core, (3, 1): 6 + core,
    }

    def tau(slot, h, r0, count, ks, width):
        first = lax.rem(chip2 + place[slot, h] + n_ab, n_ab) * pairs
        i0 = first // occ
        turn = occ * (i0 + 1) - first
        raw = slots[slot, h, r0 : r0 + count, ks].astype(F32)
        right = rtab[pl.ds(pl.multiple_of(lax.rem(first, occ) + r0, 32), count), ks]
        pair = lax.broadcasted_iota(jnp.int32, (count, width), 0) + r0
        before, after = (jnp.concatenate([ltab[i, :, ks]] * (count // 8), axis=0) for i in (i0, i0 + 1))
        left = jnp.where(pair < turn, before, after)
        return (raw + left * right).astype(BF16)

    def product(parts, out):
        total = sum(p[3] for p in parts)

        def piece(ks, width):
            formed = [tau(*p, ks, width) for p in parts]
            both = jnp.concatenate(formed, axis=0) if len(formed) > 1 else formed[0]
            return lax.dot_general(a_v[:, ks], both, (((1,), (1,)), ((), ())), preferred_element_type=F32)

        whole = cols // KC
        out[0:rows, 0:total] = piece(pl.ds(whole * KC, cols - whole * KC), cols - whole * KC)

        def step(t, carry):
            out[0:rows, 0:total] += piece(pl.ds(pl.multiple_of(t * KC, KC), KC), KC)
            return carry

        lax.fori_loop(0, whole, step, 0)

    def put(value, parts):
        lane0 = 0
        for slot, h, r0, count in parts:
            o_ref[first_k[slot, h], :, r0 : r0 + count] = value[0:take, lane0 : lane0 + count]
            lane0 += count

    def z_copy(s, k):
        to = lax.rem(z + k, N_Z)
        return remote(
            sbuf.at[s, to], rbuf.at[s, k - 1], z_s.at[s, k - 1], z_r.at[s, k - 1], {"cd": x_hi * N_Z + to}
        )

    def scatter(s):
        for j in range(n_cd):
            sbuf[s, j % N_Z, j // N_Z, :, :] = acc[j * take : j * take + 32, :].astype(sbuf.dtype)

        def send(k, carry):
            z_copy(s, k).start()
            return carry

        lax.fori_loop(1, N_Z, send, 0)

    def x_copy(s):
        return remote(xsend.at[s], xrecv.at[s], x_s.at[s], x_r.at[s], {"cd": (1 - x_hi) * N_Z + z})

    def gather(s):
        def arrive(k, carry):
            z_copy(s, k).wait_recv()
            return carry

        lax.fori_loop(1, N_Z, arrive, 0)
        for dst, xo in ((xsend, 1 - x_hi), (tot, x_hi)):
            total = sbuf[s, z, xo].astype(F32)
            for k in range(N_Z - 1):
                total = total + rbuf[s, k, xo].astype(F32)
            dst[s] = total
        x_copy(s).start()

    def finish(s, parts):
        x_copy(s).wait_recv()
        put(tot[s] + xrecv[s], parts)

    order = [(x, k) for k in (4, 3, 5, 2, 6, 1, 7, 0) for x in (1, 0) if x or k]

    def all_copies(send, recv, ss, rs):
        copies = []
        for x, k in order:
            to = lax.rem(x_hi + x, n_x) * N_Z + lax.rem(z + k, N_Z)
            n = 2 * k + x - 1
            copies.append(remote(send.at[to], recv.at[n], ss.at[n], rs.at[n], {"cd": to}))
        return copies

    def all_sum(send, recv, copies):
        for copy in reversed(copies):
            copy.wait_recv()
        value = send[cd].astype(F32)
        for n in range(n_cd - 1):
            value = value + recv[n].astype(F32)
        return value

    acc[rows:, :] = jnp.zeros((acc.shape[0] - rows, acc.shape[1]), F32)
    acc_l[rows:, :] = jnp.zeros((acc_l.shape[0] - rows, acc_l.shape[1]), F32)

    parts = [
        [(0, 0, 0, pairs), (0, 1, 0, pairs)],
        [(1, 0, 0, half), (1, 1, half, half), (2, 0, 0, half), (2, 1, half, half)],
        [(1, 0, half, half), (1, 1, 0, half), (2, 0, half, half), (2, 1, 0, half)],
    ]
    late = [(3, 1, 0, pairs), (3, 0, 0, half)]
    late_1 = [(3, 1, 0, pairs), (3, 0, 0, pairs)]
    last = [(3, 0, half, half)]

    load_d.wait()
    load_a.wait()
    own.wait_recv()
    product(parts[0], acc)
    scatter(0)

    up[0].wait_recv()
    sh_up[0].start()
    dn[0].wait_recv()
    sh_dn[0].start()
    sh_up_in = [remote(slots.at[1, 1 - core, q], slots.at[1, 1 - core, q], sib_s.at[i], sib_r.at[i], sib) for i, q in enumerate(other)]
    sh_dn_in = [remote(slots.at[2, 1 - core, q], slots.at[2, 1 - core, q], sib_s.at[2 + i], sib_r.at[2 + i], sib) for i, q in enumerate(other)]
    sh_f1_in = remote(slots.at[3, 1, part[0]], slots.at[3, 1, part[0]], sib_s.at[4], sib_r.at[4], sib)

    @pl.when(core == 0)
    def _():
        fd[0].start()
        sh_up_in[0].wait_recv()
        f1.start()
        f0.start()

    @pl.when(core == 1)
    def _():
        sh_up_in[0].wait_recv()

    sh_dn_in[0].wait_recv()
    product(parts[1], acc)
    scatter(1)

    up[1].wait_recv()
    sh_up[1].start()

    @pl.when(core == 1)
    def _():
        f1.start()

    dn[1].wait_recv()
    sh_dn[1].start()

    @pl.when(core == 0)
    def _():
        fd[1].start()

    sh_up_in[1].wait_recv()

    @pl.when(core == 1)
    def _():
        f0.start()

    sh_dn_in[1].wait_recv()
    product(parts[2], acc)
    scatter(2)
    gather(0)
    gather(1)

    f1.wait_recv()
    sh_f1.start()
    gather(2)
    h_copies = all_copies(hsend, hrecv, h_s, h_r)
    l_copies = all_copies(lsend, lrecv, l_s, l_r)

    @pl.when(core == 0)
    def _():
        f0_in[0].wait_recv()
        sh_f1_in.wait_recv()
        product(late, acc)

    @pl.when(core == 1)
    def _():
        fd_in[0].wait_recv()
        fd_in[1].wait_recv()
        sh_f1_in.wait_recv()
        product(late_1, acc)

    for j in range(n_cd):
        hsend[j, :, :] = acc[j * take : j * take + 32, :].astype(hsend.dtype)
    for copy in h_copies:
        copy.start()
    finish(0, parts[0])
    finish(1, parts[1])

    @pl.when(core == 0)
    def _():
        f0_in[1].wait_recv()
        product(last, acc_l)
        for j in range(n_cd):
            lsend[j, :, :] = jnp.concatenate(
                [acc_l[j * take + 7 * a : j * take + 7 * a + 8, :] for a in range(4)], axis=1
            )
        for copy in l_copies:
            copy.start()

    finish(2, parts[2])
    value = all_sum(hsend, hrecv, h_copies)
    put(value, late)

    @pl.when(core == 1)
    def _():
        o_ref[first_k[3, 0], :, half:pairs] = value[0:take, pairs + half : 2 * pairs]

    @pl.when(core == 0)
    def _():
        final = all_sum(lsend, lrecv, l_copies)
        for a in range(4):
            count = min(7, take - 7 * a)
            o_ref[first_k[3, 0], 7 * a : 7 * a + count, half:pairs] = final[0:count, a * half : (a + 1) * half]

    for copy in (*up, *dn, own, *sh_up, *sh_dn, f1, sh_f1, f0, *h_copies):
        copy.wait_send()

    @pl.when(core == 0)
    def _():
        for copy in (*fd, *l_copies):
            copy.wait_send()

    for s in range(3):
        x_copy(s).wait_send()

        def sent(k, carry, s=s):
            z_copy(s, k).wait_send()
            return carry

        lax.fori_loop(1, N_Z, sent, 0)


def shards(integrals, doubles, singles):
    rows, cols = integrals.shape
    pairs = doubles.shape[0]
    occ, virt = singles.shape
    n_ab, n_cd = lax.axis_size("ab"), lax.axis_size("cd")
    steps = n_ab // 4
    take = rows // n_cd
    dma = pltpu.SemaphoreType.DMA
    return pl.pallas_call(
        kernel,
        out_shape=jax.ShapeDtypeStruct((steps, take, pairs), F32),
        in_specs=[pl.BlockSpec(memory_space=pl.ANY)] * 3,
        out_specs=pl.BlockSpec(memory_space=pltpu.VMEM),
        scratch_shapes=[
            pltpu.VMEM((rows, cols), BF16),
            pltpu.VMEM((occ, virt), F32),
            pltpu.VMEM((4, 2, pairs, cols), BF16),
            pltpu.VMEM((occ + 32, cols), F32),
            pltpu.VMEM((16, 8, cols), F32),
            pltpu.VMEM((rows + 8, 2 * pairs), F32),
            pltpu.VMEM((rows + 8, pairs // 2), F32),
            pltpu.VMEM((3, N_Z, n_cd // N_Z, 32, 2 * pairs), BF16),
            pltpu.VMEM((3, N_Z - 1, n_cd // N_Z, 32, 2 * pairs), BF16),
            pltpu.VMEM((3, 32, 2 * pairs), F32),
            pltpu.VMEM((3, 32, 2 * pairs), F32),
            pltpu.VMEM((3, 32, 2 * pairs), F32),
            pltpu.VMEM((n_cd, 32, 2 * pairs), BF16),
            pltpu.VMEM((n_cd - 1, 32, 2 * pairs), BF16),
            pltpu.VMEM((n_cd, 8, 2 * pairs), F32),
            pltpu.VMEM((n_cd - 1, 8, 2 * pairs), F32),
            dma((3,)),
            dma((2,)), dma((2,)), dma((2,)), dma((2,)), dma((2,)), dma((2,)),
            dma, dma, dma, dma((2,)),
            dma((6,)), dma((6,)),
            dma((3, N_Z - 1)), dma((3, N_Z - 1)),
            dma((3,)), dma((3,)),
            dma((n_cd - 1,)), dma((n_cd - 1,)),
            dma((n_cd - 1,)), dma((n_cd - 1,)),
        ],
        compiler_params=pltpu.CompilerParams(
            collective_id=0, has_side_effects=True, vmem_limit_bytes=60 * 2**20
        ),
        cost_estimate=pl.CostEstimate(
            flops=2 * rows * cols * steps * pairs, bytes_accessed=2 * (rows + pairs) * cols, transcendentals=0
        ),
    )(integrals, doubles, singles)


def solution(mesh):
    in_specs = (P("ab", "cd"), P("ab", "cd"), P())
    out_specs = P(None, ("ab", "cd"), None)
    return jax.shard_map(shards, mesh=mesh, in_specs=in_specs, out_specs=out_specs, check_vma=False)
```

time: 68.7 us -> 58.9 us (0.86)
  Pallas kernels: 62.9 us -> 56.7 us
  local copies, waits for them, and re-layouts: 4.96 us -> 1.61 us
    pallas_call x1, Pallas kernels: 62.9 us -> 56.7 us  [shards(): pl.pallas_call(kernel, out_shape=jax.ShapeDtypeStruct((steps, take, pairs...]
    unnamed x6 -> x0, local copies, waits for them, and re-layouts: 4.25 us -> none
    pallas_call x1, local copies, waits for them, and re-layouts: 0.71 us -> 1.61 us  [shards(): pl.pallas_call(kernel, out_shape=jax.ShapeDtypeStruct((steps, take, pairs...]
where the time goes in v2:
time: 58.9 us; the launch traced here: 58.4 us
  Pallas kernels  56.7 us (96%)
  local copies, waits for them, and re-layouts  1.61 us (3%)
    pallas_call x1, Pallas kernels, shards(): pl.pallas_call(kernel, out_shape=jax.ShapeDtypeStruct((steps, take, pairs...  56.7 us
    pallas_call x1, local copies, waits for them, and re-layouts, shards(): pl.pallas_call(kernel, out_shape=jax.ShapeDtypeStruct((steps, take, pairs...  1.61 us

profile of v2, /device:TPU:6, one launch (start us, length us, event | category | flops | bytes accessed | tf_op | source)
XLA Modules:
  0.0 58.4 jit_solution(8353036496529578030)
XLA Ops:
  0.0 56.7 %shard_map.37 = f32[8,25,64]{2,1,0:T(8,128)} custom-call(bf16[400,5200]{1,0:T(8,128)(2,1)} %a_hbm.1, bf16[64,5200]{1,0:T(8,128)(2,1)} %d_hbm.1, f32[160,400]{1,0:T(8,128)} %s_hbm.1), custom_call_target="tpu_custom_call" | custom-call | flops 2129920000 | bytes 4825600 | tf_op jit(solution)/shard_map/pallas_call | solution.py:352
  56.7 1.6 %copy.4 = f32[8,25,64]{2,0,1:T(8,128)} copy(f32[8,25,64]{2,1,0:T(8,128)} %shard_map.37) | data formatting | bytes 102400 | tf_op jit(solution)/shard_map/pallas_call | solution.py:352

commit v3 on v2

--- a/solution.py
+++ b/solution.py
@@ -12,14 +12,15 @@
 BF16 = jnp.bfloat16
 N_Z = 8
 KC = 1024
+CUT = 4096
 
 
 def kernel(
     a_hbm, d_hbm, s_hbm, o_ref,
     a_v, s_v, slots, rtab, ltab, acc, acc_l,
-    sbuf, rbuf, xsend, xrecv, tot, hsend, hrecv, lsend, lrecv,
+    sbuf, rbuf, xsend, xrecv, tot, lsend, lrecv,
     loc_sem, up_s, up_r, dn_s, dn_r, fd_s, fd_r, f1_s, f1_r, f0_s, f0_r, sib_s, sib_r,
-    z_s, z_r, x_s, x_r, h_s, h_r, l_s, l_r,
+    z_s, z_r, x_s, x_r, l_s, l_r,
 ):
     pairs, cols = d_hbm.shape
     rows = a_hbm.shape[0]
@@ -71,26 +72,37 @@
 
     part = [pl.ds(pl.multiple_of(half * r, 32), half) for r in (core, 1 - core)]
     other = [pl.ds(pl.multiple_of(half * r, 32), half) for r in (1 - core, core)]
-    up = [remote(d_hbm.at[q], slots.at[1, core, q], up_s.at[i], up_r.at[i], nxt) for i, q in enumerate(part)]
+    quarter = half // 2
+    halved = [pl.ds(pl.multiple_of(half * (1 - core) + quarter * j, 16), quarter) for j in range(2)]
+    up_rows = [part[0], *halved]
+    up = [remote(d_hbm.at[q], slots.at[1, core, q], up_s.at[i], up_r.at[i], nxt) for i, q in enumerate(up_rows)]
     dn = [remote(d_hbm.at[q], slots.at[2, core, q], dn_s.at[i], dn_r.at[i], prv) for i, q in enumerate(part)]
     own = remote(d_hbm, slots.at[0, core], sib_s.at[5], sib_r.at[5], sib)
     sh_up = [remote(slots.at[1, core, q], slots.at[1, core, q], sib_s.at[i], sib_r.at[i], sib) for i, q in enumerate(part)]
     sh_dn = [remote(slots.at[2, core, q], slots.at[2, core, q], sib_s.at[2 + i], sib_r.at[2 + i], sib) for i, q in enumerate(part)]
-    f1 = remote(slots.at[1, 1, part[1]], slots.at[3, 1, part[1]], f1_s, f1_r, nxt)
+    f1 = [remote(slots.at[1, 1, q], slots.at[3, 1, q], f1_s.at[j], f1_r.at[j], nxt) for j, q in enumerate(halved)]
     sh_f1 = remote(slots.at[3, 1, part[1]], slots.at[3, 1, part[1]], sib_s.at[4], sib_r.at[4], sib)
-    f0 = remote(slots.at[1, 0, part[0]], slots.at[3, 0, part[0]], f0_s, f0_r.at[core], nxt0)
+    spans = [pl.ds(0, CUT), pl.ds(CUT, cols - CUT)]
+    f0 = [
+        remote(slots.at[1, 0, part[0], c], slots.at[3, 0, part[0], c], f0_s.at[j], f0_r.at[core, j], nxt0)
+        for j, c in enumerate(spans)
+    ]
     f0_in = [
-        remote(slots.at[1, 0, pl.ds(i * half, half)], slots.at[3, 0, pl.ds(i * half, half)], f0_s, f0_r.at[i], nxt0)
-        for i in range(2)
+        [
+            remote(slots.at[1, 0, q, c], slots.at[3, 0, q, c], f0_s.at[j], f0_r.at[i, j], nxt0)
+            for i, q in enumerate((pl.ds(0, half), pl.ds(half, half)))
+        ]
+        for j, c in enumerate(spans)
     ]
     fd = [remote(slots.at[2, core, q], slots.at[3, core, q], fd_s.at[i], fd_r.at[i], low) for i, q in enumerate(part)]
     fd_in = [remote(slots.at[2, 0, q], slots.at[3, 0, q], fd_s.at[i], fd_r.at[i], low) for i, q in enumerate(other)]
 
-    for i in range(2):
-        up[i].start()
-        dn[i].start()
-        if i == 0:
-            own.start()
+    up[0].start()
+    dn[0].start()
+    own.start()
+    up[1].start()
+    up[2].start()
+    dn[1].start()
 
     load_s.wait()
 
@@ -127,7 +139,7 @@
         left = jnp.where(pair < turn, before, after)
         return (raw + left * right).astype(BF16)
 
-    def product(parts, out):
+    def product(parts, out, start=0, stop=None):
         total = sum(p[3] for p in parts)
 
         def piece(ks, width):
@@ -135,14 +147,21 @@
             both = jnp.concatenate(formed, axis=0) if len(formed) > 1 else formed[0]
             return lax.dot_general(a_v[:, ks], both, (((1,), (1,)), ((), ())), preferred_element_type=F32)
 
-        whole = cols // KC
-        out[0:rows, 0:total] = piece(pl.ds(whole * KC, cols - whole * KC), cols - whole * KC)
-
         def step(t, carry):
             out[0:rows, 0:total] += piece(pl.ds(pl.multiple_of(t * KC, KC), KC), KC)
             return carry
 
-        lax.fori_loop(0, whole, step, 0)
+        whole = cols // KC
+        if stop is None:
+            tail = piece(pl.ds(whole * KC, cols - whole * KC), cols - whole * KC)
+            if start:
+                out[0:rows, 0:total] += tail
+            else:
+                out[0:rows, 0:total] = tail
+            lax.fori_loop(start, whole, step, 0)
+        else:
+            out[0:rows, 0:total] = piece(pl.ds(start * KC, KC), KC)
+            lax.fori_loop(start + 1, stop, step, 0)
 
     def put(value, parts):
         lane0 = 0
@@ -180,7 +199,6 @@
             for k in range(N_Z - 1):
                 total = total + rbuf[s, k, xo].astype(F32)
             dst[s] = total
-        x_copy(s).start()
 
     def finish(s, parts):
         x_copy(s).wait_recv()
@@ -212,9 +230,10 @@
         [(1, 0, 0, half), (1, 1, half, half), (2, 0, 0, half), (2, 1, half, half)],
         [(1, 0, half, half), (1, 1, 0, half), (2, 0, half, half), (2, 1, 0, half)],
     ]
-    late = [(3, 1, 0, pairs), (3, 0, 0, half)]
+    late = [(3, 1, 0, pairs)]
     late_1 = [(3, 1, 0, pairs), (3, 0, 0, pairs)]
-    last = [(3, 0, half, half)]
+    last = [(3, 0, 0, pairs)]
+    top = (take + 1) // 2
 
     load_d.wait()
     load_a.wait()
@@ -222,35 +241,44 @@
     product(parts[0], acc)
     scatter(0)
 
+    sh_up_in = [remote(slots.at[1, 1 - core, q], slots.at[1, 1 - core, q], sib_s.at[i], sib_r.at[i], sib) for i, q in enumerate(other)]
+    sh_dn_in = [remote(slots.at[2, 1 - core, q], slots.at[2, 1 - core, q], sib_s.at[2 + i], sib_r.at[2 + i], sib) for i, q in enumerate(other)]
+    sh_f1_in = remote(slots.at[3, 1, part[0]], slots.at[3, 1, part[0]], sib_s.at[4], sib_r.at[4], sib)
+
     up[0].wait_recv()
     sh_up[0].start()
     dn[0].wait_recv()
     sh_dn[0].start()
-    sh_up_in = [remote(slots.at[1, 1 - core, q], slots.at[1, 1 - core, q], sib_s.at[i], sib_r.at[i], sib) for i, q in enumerate(other)]
-    sh_dn_in = [remote(slots.at[2, 1 - core, q], slots.at[2, 1 - core, q], sib_s.at[2 + i], sib_r.at[2 + i], sib) for i, q in enumerate(other)]
-    sh_f1_in = remote(slots.at[3, 1, part[0]], slots.at[3, 1, part[0]], sib_s.at[4], sib_r.at[4], sib)
 
     @pl.when(core == 0)
     def _():
         fd[0].start()
-        sh_up_in[0].wait_recv()
-        f1.start()
-        f0.start()
-
-    @pl.when(core == 1)
-    def _():
-        sh_up_in[0].wait_recv()
+
+    sh_up_in[0].wait_recv()
+
+    @pl.when(core == 0)
+    def _():
+        f1[0].start()
+        f1[1].start()
+        f0[0].start()
+        f0[1].start()
 
     sh_dn_in[0].wait_recv()
     product(parts[1], acc)
     scatter(1)
 
     up[1].wait_recv()
+
+    @pl.when(core == 1)
+    def _():
+        f1[0].start()
+
+    up[2].wait_recv()
     sh_up[1].start()
 
     @pl.when(core == 1)
     def _():
-        f1.start()
+        f1[1].start()
 
     dn[1].wait_recv()
     sh_dn[1].start()
@@ -263,7 +291,8 @@
 
     @pl.when(core == 1)
     def _():
-        f0.start()
+        f0[0].start()
+        f0[1].start()
 
     sh_dn_in[1].wait_recv()
     product(parts[2], acc)
@@ -271,15 +300,14 @@
     gather(0)
     gather(1)
 
-    f1.wait_recv()
+    f1[0].wait_recv()
+    f1[1].wait_recv()
     sh_f1.start()
     gather(2)
-    h_copies = all_copies(hsend, hrecv, h_s, h_r)
     l_copies = all_copies(lsend, lrecv, l_s, l_r)
 
     @pl.when(core == 0)
     def _():
-        f0_in[0].wait_recv()
         sh_f1_in.wait_recv()
         product(late, acc)
 
@@ -290,40 +318,42 @@
         sh_f1_in.wait_recv()
         product(late_1, acc)
 
-    for j in range(n_cd):
-        hsend[j, :, :] = acc[j * take : j * take + 32, :].astype(hsend.dtype)
-    for copy in h_copies:
-        copy.start()
-    finish(0, parts[0])
-    finish(1, parts[1])
-
-    @pl.when(core == 0)
-    def _():
-        f0_in[1].wait_recv()
-        product(last, acc_l)
+    scatter(3)
+
+    @pl.when(core == 0)
+    def _():
+        for copy in f0_in[0]:
+            copy.wait_recv()
+        product(last, acc_l, 0, CUT // KC)
+        for copy in f0_in[1]:
+            copy.wait_recv()
+        product(last, acc_l, CUT // KC)
         for j in range(n_cd):
-            lsend[j, :, :] = jnp.concatenate(
-                [acc_l[j * take + 7 * a : j * take + 7 * a + 8, :] for a in range(4)], axis=1
-            )
+            halves = [acc_l[j * take + r : j * take + r + 16, :] for r in (0, top)]
+            lsend[j, :, :] = jnp.concatenate(halves, axis=1).astype(lsend.dtype)
         for copy in l_copies:
             copy.start()
 
-    finish(2, parts[2])
-    value = all_sum(hsend, hrecv, h_copies)
-    put(value, late)
+    f0[1].wait_send()
+    for s in range(3):
+        x_copy(s).start()
+    gather(3)
+    x_copy(3).start()
+    for s in range(3):
+        finish(s, parts[s])
+    finish(3, late)
 
     @pl.when(core == 1)
     def _():
-        o_ref[first_k[3, 0], :, half:pairs] = value[0:take, pairs + half : 2 * pairs]
+        o_ref[first_k[3, 0], :, :] = (tot[3] + xrecv[3])[0:take, pairs : 2 * pairs]
 
     @pl.when(core == 0)
     def _():
         final = all_sum(lsend, lrecv, l_copies)
-        for a in range(4):
-            count = min(7, take - 7 * a)
-            o_ref[first_k[3, 0], 7 * a : 7 * a + count, half:pairs] = final[0:count, a * half : (a + 1) * half]
-
-    for copy in (*up, *dn, own, *sh_up, *sh_dn, f1, sh_f1, f0, *h_copies):
+        o_ref[first_k[3, 0], 0:top, :] = final[0:top, 0:pairs]
+        o_ref[first_k[3, 0], top:take, :] = final[0 : take - top, pairs : 2 * pairs]
+
+    for copy in (*up, *dn, own, *sh_up, *sh_dn, *f1, sh_f1, f0[0]):
         copy.wait_send()
 
     @pl.when(core == 0)
@@ -331,7 +361,7 @@
         for copy in (*fd, *l_copies):
             copy.wait_send()
 
-    for s in range(3):
+    for s in range(4):
         x_copy(s).wait_send()
 
         def sent(k, carry, s=s):
@@ -361,23 +391,20 @@
             pltpu.VMEM((occ + 32, cols), F32),
             pltpu.VMEM((16, 8, cols), F32),
             pltpu.VMEM((rows + 8, 2 * pairs), F32),
-            pltpu.VMEM((rows + 8, pairs // 2), F32),
-            pltpu.VMEM((3, N_Z, n_cd // N_Z, 32, 2 * pairs), BF16),
-            pltpu.VMEM((3, N_Z - 1, n_cd // N_Z, 32, 2 * pairs), BF16),
-            pltpu.VMEM((3, 32, 2 * pairs), F32),
-            pltpu.VMEM((3, 32, 2 * pairs), F32),
-            pltpu.VMEM((3, 32, 2 * pairs), F32),
-            pltpu.VMEM((n_cd, 32, 2 * pairs), BF16),
-            pltpu.VMEM((n_cd - 1, 32, 2 * pairs), BF16),
-            pltpu.VMEM((n_cd, 8, 2 * pairs), F32),
-            pltpu.VMEM((n_cd - 1, 8, 2 * pairs), F32),
+            pltpu.VMEM((rows + 8, pairs), F32),
+            pltpu.VMEM((4, N_Z, n_cd // N_Z, 32, 2 * pairs), BF16),
+            pltpu.VMEM((4, N_Z - 1, n_cd // N_Z, 32, 2 * pairs), BF16),
+            pltpu.VMEM((4, 32, 2 * pairs), F32),
+            pltpu.VMEM((4, 32, 2 * pairs), F32),
+            pltpu.VMEM((4, 32, 2 * pairs), F32),
+            pltpu.VMEM((n_cd, 16, 2 * pairs), BF16),
+            pltpu.VMEM((n_cd - 1, 16, 2 * pairs), BF16),
             dma((3,)),
-            dma((2,)), dma((2,)), dma((2,)), dma((2,)), dma((2,)), dma((2,)),
-            dma, dma, dma, dma((2,)),
+            dma((3,)), dma((3,)), dma((2,)), dma((2,)), dma((2,)), dma((2,)),
+            dma((2,)), dma((2,)), dma((2,)), dma((2, 2)),
             dma((6,)), dma((6,)),
-            dma((3, N_Z - 1)), dma((3, N_Z - 1)),
-            dma((3,)), dma((3,)),
-            dma((n_cd - 1,)), dma((n_cd - 1,)),
+            dma((4, N_Z - 1)), dma((4, N_Z - 1)),
+            dma((4,)), dma((4,)),
             dma((n_cd - 1,)), dma((n_cd - 1,)),
         ],
         compiler_params=pltpu.CompilerParams(

time: 58.9 us -> 56.7 us (0.963)
  Pallas kernels: 56.7 us -> 54.4 us
    pallas_call x1, Pallas kernels: 56.7 us -> 54.4 us  [shards(): pl.pallas_call(kernel, out_shape=jax.ShapeDtypeStruct((steps, take, pairs...]
where the time goes in v3:
time: 56.7 us; the launch traced here: 56 us
  Pallas kernels  54.4 us (96%)
  local copies, waits for them, and re-layouts  1.61 us (3%)
    pallas_call x1, Pallas kernels, shards(): pl.pallas_call(kernel, out_shape=jax.ShapeDtypeStruct((steps, take, pairs...  54.4 us
    pallas_call x1, local copies, waits for them, and re-layouts, shards(): pl.pallas_call(kernel, out_shape=jax.ShapeDtypeStruct((steps, take, pairs...  1.61 us

profile of v3, /device:TPU:6, one launch (start us, length us, event | category | flops | bytes accessed | tf_op | source)
XLA Modules:
  0.0 56.0 jit_solution(986567665567385750)
XLA Ops:
  0.0 54.4 %shard_map.37 = f32[8,25,64]{2,1,0:T(8,128)} custom-call(bf16[400,5200]{1,0:T(8,128)(2,1)} %a_hbm.1, bf16[64,5200]{1,0:T(8,128)(2,1)} %d_hbm.1, f32[160,400]{1,0:T(8,128)} %s_hbm.1), custom_call_target="tpu_custom_call" | custom-call | flops 2129920000 | bytes 4825600 | tf_op jit(solution)/shard_map/pallas_call | solution.py:382
  54.4 1.6 %copy.4 = f32[8,25,64]{2,0,1:T(8,128)} copy(f32[8,25,64]{2,1,0:T(8,128)} %shard_map.37) | data formatting | bytes 102400 | tf_op jit(solution)/shard_map/pallas_call | solution.py:382

commit v4 on v3

--- a/solution.py
+++ b/solution.py
@@ -12,6 +12,7 @@
 BF16 = jnp.bfloat16
 N_Z = 8
 KC = 1024
+VMEM_GRANT = 53 * 2**20 + 704 * 2**10
 CUT = 4096
 
 
@@ -179,11 +180,8 @@
         for j in range(n_cd):
             sbuf[s, j % N_Z, j // N_Z, :, :] = acc[j * take : j * take + 32, :].astype(sbuf.dtype)
 
-        def send(k, carry):
+        for k in (4, 3, 5, 2, 6, 1, 7):
             z_copy(s, k).start()
-            return carry
-
-        lax.fori_loop(1, N_Z, send, 0)
 
     def x_copy(s):
         return remote(xsend.at[s], xrecv.at[s], x_s.at[s], x_r.at[s], {"cd": (1 - x_hi) * N_Z + z})
@@ -303,7 +301,6 @@
     f1[0].wait_recv()
     f1[1].wait_recv()
     sh_f1.start()
-    gather(2)
     l_copies = all_copies(lsend, lrecv, l_s, l_r)
 
     @pl.when(core == 0)
@@ -319,6 +316,7 @@
         product(late_1, acc)
 
     scatter(3)
+    gather(2)
 
     @pl.when(core == 0)
     def _():
@@ -339,9 +337,27 @@
         x_copy(s).start()
     gather(3)
     x_copy(3).start()
+
+    for copy in (*up, *dn, own, *sh_up, *sh_dn, *f1, sh_f1, f0[0]):
+        copy.wait_send()
+
+    @pl.when(core == 0)
+    def _():
+        for copy in (*fd, *l_copies):
+            copy.wait_send()
+
+    for s in range(4):
+
+        def sent(k, carry, s=s):
+            z_copy(s, k).wait_send()
+            return carry
+
+        lax.fori_loop(1, N_Z, sent, 0)
     for s in range(3):
         finish(s, parts[s])
     finish(3, late)
+    for s in range(4):
+        x_copy(s).wait_send()
 
     @pl.when(core == 1)
     def _():
@@ -352,23 +368,6 @@
         final = all_sum(lsend, lrecv, l_copies)
         o_ref[first_k[3, 0], 0:top, :] = final[0:top, 0:pairs]
         o_ref[first_k[3, 0], top:take, :] = final[0 : take - top, pairs : 2 * pairs]
-
-    for copy in (*up, *dn, own, *sh_up, *sh_dn, *f1, sh_f1, f0[0]):
-        copy.wait_send()
-
-    @pl.when(core == 0)
-    def _():
-        for copy in (*fd, *l_copies):
-            copy.wait_send()
-
-    for s in range(4):
-        x_copy(s).wait_send()
-
-        def sent(k, carry, s=s):
-            z_copy(s, k).wait_send()
-            return carry
-
-        lax.fori_loop(1, N_Z, sent, 0)
 
 
 def shards(integrals, doubles, singles):
@@ -408,7 +407,7 @@
             dma((n_cd - 1,)), dma((n_cd - 1,)),
         ],
         compiler_params=pltpu.CompilerParams(
-            collective_id=0, has_side_effects=True, vmem_limit_bytes=60 * 2**20
+            collective_id=0, has_side_effects=True, vmem_limit_bytes=VMEM_GRANT
         ),
         cost_estimate=pl.CostEstimate(
             flops=2 * rows * cols * steps * pairs, bytes_accessed=2 * (rows + pairs) * cols, transcendentals=0

time: 56.7 us -> 54.2 us (0.956); the launches traced: 56 us -> 54.1 us
  Pallas kernels: 54.4 us -> 53.4 us
  local copies, waits for them, and re-layouts: 1.61 us -> 0.71 us
    pallas_call x1, Pallas kernels: 54.4 us -> 53.4 us  [shards(): pl.pallas_call(kernel, out_shape=jax.ShapeDtypeStruct((steps, take, pairs...]
    pallas_call x1, local copies, waits for them, and re-layouts: 1.61 us -> 0.71 us  [shards(): pl.pallas_call(kernel, out_shape=jax.ShapeDtypeStruct((steps, take, pairs...]
where the time goes in v4:
time: 54.2 us; the launch traced here: 54.1 us
  Pallas kernels  53.4 us (99%)
  local copies, waits for them, and re-layouts  0.71 us (1%)
    pallas_call x1, Pallas kernels, shards(): pl.pallas_call(kernel, out_shape=jax.ShapeDtypeStruct((steps, take, pairs...  53.4 us

profile of v4, /device:TPU:6, one launch (start us, length us, event | category | flops | bytes accessed | tf_op | source)
XLA Modules:
  0.0 54.1 jit_solution(13746203323355993641)
XLA Ops:
  0.0 53.4 %shard_map.37 = f32[8,25,64]{2,1,0:T(8,128)S(1)} custom-call(bf16[400,5200]{1,0:T(8,128)(2,1)} %a_hbm.1, bf16[64,5200]{1,0:T(8,128)(2,1)} %d_hbm.1, f32[160,400]{1,0:T(8,128)} %s_hbm.1), custom_call_target="tpu_custom_call" | custom-call | flops 2129920000 | bytes 4825600 | tf_op jit(solution)/shard_map/pallas_call | solution.py:381
  53.4 0.7 %copy.4 = f32[8,25,64]{2,0,1:T(8,128)} copy(f32[8,25,64]{2,1,0:T(8,128)S(1)} %shard_map.37) | data formatting | bytes 102400 | tf_op jit(solution)/shard_map/pallas_call | solution.py:381

commit v5 on v4

--- a/solution.py
+++ b/solution.py
@@ -11,9 +11,9 @@
 F32 = jnp.float32
 BF16 = jnp.bfloat16
 N_Z = 8
-KC = 1024
+KC = 2048
 VMEM_GRANT = 53 * 2**20 + 704 * 2**10
-CUT = 4096
+CUTS = (0, 2048, 4096)
 
 
 def kernel(
@@ -60,8 +60,8 @@
     load_s = pltpu.make_async_copy(s_hbm, s_v, loc_sem.at[0])
     load_d = pltpu.make_async_copy(d_hbm, slots.at[0, core], loc_sem.at[1])
     load_a = pltpu.make_async_copy(a_hbm, a_v, loc_sem.at[2])
+    load_d.start()
     load_s.start()
-    load_d.start()
     load_a.start()
 
     pl.semaphore_wait(bar, n_cd + 3)
@@ -76,14 +76,15 @@
     quarter = half // 2
     halved = [pl.ds(pl.multiple_of(half * (1 - core) + quarter * j, 16), quarter) for j in range(2)]
     up_rows = [part[0], *halved]
-    up = [remote(d_hbm.at[q], slots.at[1, core, q], up_s.at[i], up_r.at[i], nxt) for i, q in enumerate(up_rows)]
-    dn = [remote(d_hbm.at[q], slots.at[2, core, q], dn_s.at[i], dn_r.at[i], prv) for i, q in enumerate(part)]
-    own = remote(d_hbm, slots.at[0, core], sib_s.at[5], sib_r.at[5], sib)
+    up = [remote(slots.at[0, core, q], slots.at[1, core, q], up_s.at[i], up_r.at[i], nxt) for i, q in enumerate(up_rows)]
+    dn = [remote(slots.at[0, core, q], slots.at[2, core, q], dn_s.at[i], dn_r.at[i], prv) for i, q in enumerate(part)]
+    own = remote(slots.at[0, core], slots.at[0, core], sib_s.at[5], sib_r.at[5], sib)
     sh_up = [remote(slots.at[1, core, q], slots.at[1, core, q], sib_s.at[i], sib_r.at[i], sib) for i, q in enumerate(part)]
     sh_dn = [remote(slots.at[2, core, q], slots.at[2, core, q], sib_s.at[2 + i], sib_r.at[2 + i], sib) for i, q in enumerate(part)]
     f1 = [remote(slots.at[1, 1, q], slots.at[3, 1, q], f1_s.at[j], f1_r.at[j], nxt) for j, q in enumerate(halved)]
-    sh_f1 = remote(slots.at[3, 1, part[1]], slots.at[3, 1, part[1]], sib_s.at[4], sib_r.at[4], sib)
-    spans = [pl.ds(0, CUT), pl.ds(CUT, cols - CUT)]
+    sh_f1 = [remote(slots.at[3, 1, q], slots.at[3, 1, q], sib_s.at[j], sib_r.at[j], sib) for j, q in zip((4, 6), halved)]
+    ends = (*CUTS[1:], cols)
+    spans = [pl.ds(a, b - a) for a, b in zip(CUTS, ends)]
     f0 = [
         remote(slots.at[1, 0, part[0], c], slots.at[3, 0, part[0], c], f0_s.at[j], f0_r.at[core, j], nxt0)
         for j, c in enumerate(spans)
@@ -98,6 +99,7 @@
     fd = [remote(slots.at[2, core, q], slots.at[3, core, q], fd_s.at[i], fd_r.at[i], low) for i, q in enumerate(part)]
     fd_in = [remote(slots.at[2, 0, q], slots.at[3, 0, q], fd_s.at[i], fd_r.at[i], low) for i, q in enumerate(other)]
 
+    load_d.wait()
     up[0].start()
     dn[0].start()
     own.start()
@@ -124,6 +126,8 @@
 
     far = jnp.where(core == 0, -4, 4)
     place = {(0, 0): 0, (0, 1): 1, (1, 0): -2, (1, 1): -1, (2, 0): 2, (2, 1): 3, (3, 0): far, (3, 1): -3}
+    row = lax.rem(ab // 2, n_ab // 4)
+    inner = jnp.logical_and(row > 0, row < n_ab // 4 - 1)
     first_k = {
         (0, 0): 3 + core, (0, 1): 2 + core, (1, 0): 5 + core, (1, 1): 4 + core,
         (2, 0): 1 + core, (2, 1): core, (3, 0): 7 - 7 * core, (3, 1): 6 + core,
@@ -161,8 +165,9 @@
                 out[0:rows, 0:total] = tail
             lax.fori_loop(start, whole, step, 0)
         else:
-            out[0:rows, 0:total] = piece(pl.ds(start * KC, KC), KC)
-            lax.fori_loop(start + 1, stop, step, 0)
+            if start == 0:
+                out[0:rows, 0:total] = piece(pl.ds(0, KC), KC)
+            lax.fori_loop(max(start, 1), stop, step, 0)
 
     def put(value, parts):
         lane0 = 0
@@ -197,6 +202,10 @@
             for k in range(N_Z - 1):
                 total = total + rbuf[s, k, xo].astype(F32)
             dst[s] = total
+
+        @pl.when(jnp.logical_and(inner, s < 3))
+        def _():
+            x_copy(s).start()
 
     def finish(s, parts):
         x_copy(s).wait_recv()
@@ -233,7 +242,6 @@
     last = [(3, 0, 0, pairs)]
     top = (take + 1) // 2
 
-    load_d.wait()
     load_a.wait()
     own.wait_recv()
     product(parts[0], acc)
@@ -241,7 +249,8 @@
 
     sh_up_in = [remote(slots.at[1, 1 - core, q], slots.at[1, 1 - core, q], sib_s.at[i], sib_r.at[i], sib) for i, q in enumerate(other)]
     sh_dn_in = [remote(slots.at[2, 1 - core, q], slots.at[2, 1 - core, q], sib_s.at[2 + i], sib_r.at[2 + i], sib) for i, q in enumerate(other)]
-    sh_f1_in = remote(slots.at[3, 1, part[0]], slots.at[3, 1, part[0]], sib_s.at[4], sib_r.at[4], sib)
+    theirs = [pl.ds(pl.multiple_of(half * core + quarter * j, 16), quarter) for j in range(2)]
+    sh_f1_in = [remote(slots.at[3, 1, q], slots.at[3, 1, q], sib_s.at[j], sib_r.at[j], sib) for j, q in zip((4, 6), theirs)]
 
     up[0].wait_recv()
     sh_up[0].start()
@@ -258,8 +267,8 @@
     def _():
         f1[0].start()
         f1[1].start()
-        f0[0].start()
-        f0[1].start()
+        for copy in f0:
+            copy.start()
 
     sh_dn_in[0].wait_recv()
     product(parts[1], acc)
@@ -289,8 +298,8 @@
 
     @pl.when(core == 1)
     def _():
-        f0[0].start()
-        f0[1].start()
+        for copy in f0:
+            copy.start()
 
     sh_dn_in[1].wait_recv()
     product(parts[2], acc)
@@ -298,21 +307,23 @@
     gather(0)
     gather(1)
 
-    f1[0].wait_recv()
-    f1[1].wait_recv()
-    sh_f1.start()
+    for j in range(2):
+        f1[j].wait_recv()
+        sh_f1[j].start()
     l_copies = all_copies(lsend, lrecv, l_s, l_r)
 
     @pl.when(core == 0)
     def _():
-        sh_f1_in.wait_recv()
+        for copy in sh_f1_in:
+            copy.wait_recv()
         product(late, acc)
 
     @pl.when(core == 1)
     def _():
         fd_in[0].wait_recv()
         fd_in[1].wait_recv()
-        sh_f1_in.wait_recv()
+        for copy in sh_f1_in:
+            copy.wait_recv()
         product(late_1, acc)
 
     scatter(3)
@@ -320,25 +331,39 @@
 
     @pl.when(core == 0)
     def _():
-        for copy in f0_in[0]:
-            copy.wait_recv()
-        product(last, acc_l, 0, CUT // KC)
-        for copy in f0_in[1]:
-            copy.wait_recv()
-        product(last, acc_l, CUT // KC)
+        for j, copies in enumerate(f0_in):
+            for copy in copies:
+                copy.wait_recv()
+            product(last, acc_l, CUTS[j] // KC, ends[j] // KC if j + 1 < len(CUTS) else None)
         for j in range(n_cd):
             halves = [acc_l[j * take + r : j * take + r + 16, :] for r in (0, top)]
             lsend[j, :, :] = jnp.concatenate(halves, axis=1).astype(lsend.dtype)
-        for copy in l_copies:
-            copy.start()
-
-    f0[1].wait_send()
-    for s in range(3):
-        x_copy(s).start()
+        def send(t, carry):
+            x = n_x - 1 - lax.rem(t, n_x)
+            k = lax.rem(t // n_x - z + N_Z, N_Z)
+
+            @pl.when(x + k > 0)
+            def _():
+                to = lax.rem(x_hi + x, n_x) * N_Z + t // n_x
+                n = n_x * k + x - 1
+                remote(lsend.at[to], lrecv.at[n], l_s.at[n], l_r.at[n], {"cd": to}).start()
+
+            return carry
+
+        lax.fori_loop(0, n_cd, send, 0)
+
+    for copy in f0:
+        copy.wait_send()
+
+    @pl.when(jnp.logical_not(inner))
+    def _():
+        for s in range(3):
+            x_copy(s).start()
+
     gather(3)
     x_copy(3).start()
 
-    for copy in (*up, *dn, own, *sh_up, *sh_dn, *f1, sh_f1, f0[0]):
+    for copy in (*up, *dn, own, *sh_up, *sh_dn, *f1, *sh_f1):
         copy.wait_send()
 
     @pl.when(core == 0)
@@ -400,8 +425,8 @@
             pltpu.VMEM((n_cd - 1, 16, 2 * pairs), BF16),
             dma((3,)),
             dma((3,)), dma((3,)), dma((2,)), dma((2,)), dma((2,)), dma((2,)),
-            dma((2,)), dma((2,)), dma((2,)), dma((2, 2)),
-            dma((6,)), dma((6,)),
+            dma((2,)), dma((2,)), dma((len(CUTS),)), dma((2, len(CUTS))),
+            dma((7,)), dma((7,)),
             dma((4, N_Z - 1)), dma((4, N_Z - 1)),
             dma((4,)), dma((4,)),
             dma((n_cd - 1,)), dma((n_cd - 1,)),

time: 54.2 us -> 53.5 us (0.987)
  Pallas kernels: 53.4 us -> 52.7 us
    pallas_call x1, Pallas kernels: 53.4 us -> 52.7 us  [shards(): pl.pallas_call(kernel, out_shape=jax.ShapeDtypeStruct((steps, take, pairs...]
where the time goes in v5:
time: 53.5 us; the launch traced here: 53.4 us
  Pallas kernels  52.7 us (99%)
  local copies, waits for them, and re-layouts  0.71 us (1%)
    pallas_call x1, Pallas kernels, shards(): pl.pallas_call(kernel, out_shape=jax.ShapeDtypeStruct((steps, take, pairs...  52.7 us

profile of v5, /device:TPU:6, one launch (start us, length us, event | category | flops | bytes accessed | tf_op | source)
XLA Modules:
  0.0 53.4 jit_solution(16435842020613640702)
XLA Ops:
  0.0 52.7 %shard_map.37 = f32[8,25,64]{2,1,0:T(8,128)S(1)} custom-call(bf16[400,5200]{1,0:T(8,128)(2,1)} %a_hbm.1, bf16[64,5200]{1,0:T(8,128)(2,1)} %d_hbm.1, f32[160,400]{1,0:T(8,128)} %s_hbm.1), custom_call_target="tpu_custom_call" | custom-call | flops 2129920000 | bytes 4825600 | tf_op jit(solution)/shard_map/pallas_call | solution.py:406
  52.7 0.7 %copy.4 = f32[8,25,64]{2,0,1:T(8,128)} copy(f32[8,25,64]{2,1,0:T(8,128)S(1)} %shard_map.37) | data formatting | bytes 102400 | tf_op jit(solution)/shard_map/pallas_call | solution.py:406

commit v6 on v5

--- a/solution.py
+++ b/solution.py
@@ -51,11 +51,12 @@
     for peer in (nxt, prv, low, high):
         pl.semaphore_signal(bar, inc=1, device_id=peer, device_id_type=MESH)
 
-    def greet(k, carry):
-        pl.semaphore_signal(bar, inc=1, device_id={"cd": lax.rem(cd + k, n_cd)}, device_id_type=MESH)
-        return carry
-
-    lax.fori_loop(1, n_cd, greet, 0)
+    for k in (0, 1, 7, 2, 6, 3, 5, 4):
+        for x in (1, 0):
+            if x or k:
+                member = {"cd": lax.rem(x_hi + x, n_x) * N_Z + lax.rem(z + k, N_Z)}
+                pl.semaphore_signal(bar, inc=1, device_id=member, device_id_type=MESH)
+
 
     load_s = pltpu.make_async_copy(s_hbm, s_v, loc_sem.at[0])
     load_d = pltpu.make_async_copy(d_hbm, slots.at[0, core], loc_sem.at[1])

time: 53.5 us -> 53.7 us (level)
  no operation moved by 1% of the time
where the time goes in v6:
time: 53.7 us; the launch traced here: 53.6 us
  Pallas kernels  52.9 us (99%)
  local copies, waits for them, and re-layouts  0.71 us (1%)
    pallas_call x1, Pallas kernels, shards(): pl.pallas_call(kernel, out_shape=jax.ShapeDtypeStruct((steps, take, pairs...  52.9 us

profile of v6, /device:TPU:6, one launch (start us, length us, event | category | flops | bytes accessed | tf_op | source)
XLA Modules:
  0.0 53.6 jit_solution(10570721387270323671)
XLA Ops:
  0.0 52.9 %shard_map.37 = f32[8,25,64]{2,1,0:T(8,128)S(1)} custom-call(bf16[400,5200]{1,0:T(8,128)(2,1)} %a_hbm.1, bf16[64,5200]{1,0:T(8,128)(2,1)} %d_hbm.1, f32[160,400]{1,0:T(8,128)} %s_hbm.1), custom_call_target="tpu_custom_call" | custom-call | flops 2129920000 | bytes 4825600 | tf_op jit(solution)/shard_map/pallas_call | solution.py:407
  52.9 0.7 %copy.4 = f32[8,25,64]{2,0,1:T(8,128)} copy(f32[8,25,64]{2,1,0:T(8,128)S(1)} %shard_map.37) | data formatting | bytes 102400 | tf_op jit(solution)/shard_map/pallas_call | solution.py:407
